TPU v7x, 768 devices: a whole 4x8x12 slice. The times are simulated.
768 devices in a mesh: blk: 64 (over y, x, core), sig: 12 (over z).
Axes of the slice: x: 4, y: 8, z: 12, core: 2. Of those that a mesh axis runs over, the one named last changes fastest.
Arguments:
- coarse_fields: float32 [98304, 3, 512], P(('blk', 'sig')), may hold values from -6 to 6
- fine_fields: float32 [24576, 3, 8, 512], P(('blk', 'sig')), may hold values from -6 to 6
- owner: int32 [24576, 1], P(('blk', 'sig')), may hold values from 0 to 63, as said below
- target_tile: int32 [24576, 1], P(('blk', 'sig')), may hold values from 0 to 127, as said below
- tags: int32 [98304, 512], P(('blk', 'sig')), may hold values 0 or 1
Outputs:
- synced: float32 [98304, 3, 512], P(('blk', 'sig'))
- signature: float32 [64, 1032], P('blk')
Inputs may be any that keep to these rules, and one draw needn't show every extreme that they name: On the 32 patches of one device at most 2 name the same owner; in every sig slab some devices name one owner exactly 2 times. `target_tile`: among the patches of all devices with one sig index no owner and tile is named twice; in every sig slab one owner has all 128 of its tiles named.
All inputs are finite; a program needn't handle non-finite values. No bound on the sum of `tags` on one device may be relied on, other than what follows from the above.
Results may differ from a plain program's by a relative error of at most 0.0002.
Values sent between devices are 32-bit elements; how exact they have to be, the bound alone decides.
No kernel may reach another device: no remote copies, remote signals or barrier semaphores. Data moves between devices by JAX's collectives and lax.ppermute only.
A program may use at most 32 MiB of HBM per device.

v0:
```python
import jax
import jax.numpy as jnp
from jax import lax
from jax.sharding import PartitionSpec as P

EDGE = 8


def indicator_of(fields):
    edge_len = fields.shape[2]
    total = jnp.zeros(fields.shape[:1] + fields.shape[2:], jnp.float32)
    for axis_number in (2, 3, 4):
        upper = lax.slice_in_dim(fields, 2, edge_len, axis=axis_number)
        lower = lax.slice_in_dim(fields, 0, edge_len - 2, axis=axis_number)
        middle = 0.5 * (upper - lower)
        widths = [(0, 0)] * 5
        widths[axis_number] = (1, 1)
        padded = jnp.pad(middle, widths)
        total = total + jnp.sum(padded * padded, axis=1)
    return total


def shards(coarse_fields, fine_fields, owner, target_tile, tags):
    patch_count = fine_fields.shape[0]
    tile_count = coarse_fields.shape[0]
    cell_count = coarse_fields.shape[2]
    edge_len = EDGE
    width = 3 * cell_count
    blocks = lax.axis_size("blk")
    slabs = lax.axis_size("sig")
    destination = owner[:, 0]
    target = target_tile[:, 0]
    child_mean = 0.125 * jnp.sum(fine_fields, axis=2)
    averaged = child_mean.reshape(patch_count, width)
    capacity = max(2, (tile_count + blocks - 1) // blocks)
    dest_match = (destination[:, None] == jnp.arange(blocks, dtype=jnp.int32)[None, :]).astype(
        jnp.int32
    )
    before = jnp.cumsum(dest_match, axis=0) - dest_match
    slot_rank = jnp.sum(before * dest_match, axis=1)
    slot_index = destination * capacity + slot_rank
    send_data = jnp.zeros((blocks * capacity, width), jnp.float32).at[slot_index].set(averaged)
    send_tiles = (
        jnp.zeros((blocks * capacity,), jnp.float32)
        .at[slot_index]
        .set((target + 1).astype(jnp.float32))
    )
    got_data, got_tiles = (
        lax.all_to_all(
            send_data.reshape(blocks, capacity, width),
            "blk",
            split_axis=0,
            concat_axis=0,
            tiled=True,
        ),
        lax.all_to_all(
            send_tiles.reshape(blocks, capacity), "blk", split_axis=0, concat_axis=0, tiled=True
        ),
    )
    tile_of_slot = got_tiles.reshape(blocks * capacity).astype(jnp.int32) - 1
    tile_of_slot = jnp.where(tile_of_slot < 0, tile_count, tile_of_slot)
    totals = (
        jnp.zeros((tile_count, width), jnp.float32)
        .at[tile_of_slot]
        .set(got_data.reshape(blocks * capacity, width), mode="drop")
    )
    covered = jnp.zeros((tile_count,), jnp.float32).at[tile_of_slot].set(1.0, mode="drop")
    flat = coarse_fields.reshape(tile_count, width)
    synced = jnp.where(covered[:, None] > 0, totals, flat)
    synced = synced.reshape(tile_count, 3, cell_count)
    indicator = indicator_of(synced.reshape(tile_count, 3, edge_len, edge_len, edge_len))
    weight = tags.reshape(tile_count, edge_len, edge_len, edge_len).astype(jnp.float32) * indicator
    part_y = jnp.sum(weight, axis=(1, 3)).reshape(tile_count * edge_len)
    part_z = jnp.sum(weight, axis=(0, 1, 2))
    sum_y, sum_z = lax.psum((part_y, part_z), "sig")
    along_y = sum_y / (edge_len * edge_len * slabs)
    along_z = sum_z / (edge_len * edge_len * tile_count * slabs)
    signature = jnp.concatenate([along_y, along_z])[None, :]
    return (synced, signature)


def solution(mesh):
    return jax.shard_map(
        shards,
        mesh=mesh,
        in_specs=(
            P(("blk", "sig"), None, None),
            P(("blk", "sig"), None, None, None),
            P(("blk", "sig"), None),
            P(("blk", "sig"), None),
            P(("blk", "sig"), None),
        ),
        out_specs=(P(("blk", "sig"), None, None), P("blk", None)),
        check_vma=False,
    )
```

profile of v0, /device:TPU:4, one launch (start us, length us, event | category | flops | bytes accessed | tf_op | source)
XLA Modules:
  0.0 91.5 jit_solution(5788183323938558442)
XLA Ops:
  0.6 0.7 fusion.8
  1.4 0.1 reduce_window_sum.11
  1.4 0.8 select_reduce_fusion
  2.2 0.7 fusion.9
  2.9 0.7 scatter_custom_fusion
  3.6 0.7 all_to_all.9
  4.4 13.6 %all-to-all-start = ((f32[64,1,2]{2,1,0:T(1,128)}), f32[64,1,2]{2,1,0:T(1,128)S(1)}, u32[]{:S(2)}, u32[]{:S(2)}) async-start(f32[64,1,2]{2,1,0:T(1,128)} %bitcast.4), calls=%async_computation | async-start | bytes 65536 | tf_op jit(solution)/shard_map/all_to_all | solution.py:56
  17.9 1.9 %reduce_sum.74 = f32[32,3,512]{2,1,0:T(4,128)S(1)} reduce(f32[32,3,8,512]{3,2,1,0:T(8,128)} %param.6, f32[]{:T(128)} %constant.11.clone.1), dimensions={2}, to_apply=%region_4.5 | reduce | flops 344064 | bytes 1769476 | tf_op jit(solution)/shard_map/reduce_sum | solution.py:33
  19.8 0.1 broadcast_multiply_fusion
  19.9 0.1 copy.32
  20.0 0.9 %scatter_custom_fusion.2 = f32[128,1536]{1,0:T(8,128)S(1)} fusion(s32[32]{0:T(128)S(1)} %get-tuple-element.14, f32[32,1536]{1,0:T(8,128)S(1)} %bitcast.29, f32[]{:T(128)} %constant.11.clone.1), kind=kCustom, calls=%fused_computation.15 | custom fusion | bytes 786436 | tf_op jit(solution)/shard_map/scatter | solution.py:42
  20.9 0.0 copy-start
  20.9 1.3 %reshape.74 = f32[64,2,1536]{2,1,0:T(2,128)} reshape(f32[128,1536]{1,0:T(8,128)S(1)} %scatter_custom_fusion.2) | data formatting | bytes 1572864 | tf_op jit(solution)/shard_map/reshape | solution.py:50
  22.2 3.6 %all-to-all-done = f32[64,1,2]{2,1,0:T(1,128)S(1)} async-done(((f32[64,1,2]{2,1,0:T(1,128)}), f32[64,1,2]{2,1,0:T(1,128)S(1)}, u32[]{:S(2)}, u32[]{:S(2)}) %all-to-all-start) | async-done | bytes 544 | tf_op jit(solution)/shard_map/all_to_all | solution.py:56
  25.8 6.8 %all-to-all-start.1 = ((f32[64,2,1536]{2,1,0:T(2,128)}), f32[64,2,1536]{2,1,0:T(2,128)S(1)}, u32[]{:S(2)}, u32[]{:S(2)}) async-start(f32[64,2,1536]{2,1,0:T(2,128)} %reshape.74), calls=%async_computation.1 | async-start | bytes 1572864 | tf_op jit(solution)/shard_map/all_to_all | solution.py:49
  32.6 0.0 copy-done
  32.6 0.0 copy-start.1
  32.7 0.3 copy.25
  32.9 0.3 copy.26
  33.2 0.4 copy-done.1
  33.6 0.1 copy.28
  33.8 0.1 add_reduce_fusion
  33.9 0.1 sub.20
  34.0 1.0 %scatter_custom_fusion.1 = f32[128]{0:T(128)S(1)} fusion(s32[128]{0:T(128)S(1)} %fusion.10, f32[128]{0:T(128)S(1)} %broadcast.88, f32[]{:T(128)} %constant.11.clone.1), kind=kCustom, calls=%fused_computation.38 | custom fusion | bytes 516 | tf_op jit(solution)/shard_map/scatter | solution.py:67
  35.0 20.8 %all-to-all-done.1 = f32[64,2,1536]{2,1,0:T(2,128)S(1)} async-done(((f32[64,2,1536]{2,1,0:T(2,128)}), f32[64,2,1536]{2,1,0:T(2,128)S(1)}, u32[]{:S(2)}, u32[]{:S(2)}) %all-to-all-start.1) | async-done | bytes 786464 | tf_op jit(solution)/shard_map/all_to_all | solution.py:49
  55.8 0.5 reshape.107
  56.4 1.3 %scatter_custom_fusion.3 = f32[128,1536]{1,0:T(8,128)S(1)} fusion(s32[128]{0:T(128)S(1)} %fusion.10, f32[128,1536]{1,0:T(8,128)S(1)} %reshape.107, f32[]{:T(128)} %constant.11.clone.1), kind=kCustom, calls=%fused_computation.13 | custom fusion | bytes 786436 | tf_op jit(solution)/shard_map/scatter | solution.py:65
  57.7 0.1 broadcast_select_fusion
  57.8 0.3 copy.27
  58.1 0.1 fusion
  58.2 0.1 fusion.1
  58.3 0.1 fusion.2
  58.3 0.1 multiply_reduce_fusion
  58.5 0.1 multiply_reduce_fusion.3
  58.6 0.1 copy.30
  58.7 0.1 reshape.78
  58.8 0.1 fusion.7
  59.0 0.1 reduce_sum.80
  59.1 30.6 %all-reduce.3 = (f32[8]{0:T(128)S(1)}, f32[1024]{0:T(1024)S(1)}) all-reduce(f32[8]{0:T(128)S(1)} %reduce_sum.81, f32[1024]{0:T(1024)S(1)} %reshape.78), channel_id=1, replica_groups=mesh['blk'=64,'sig'=12] {'sig'}, use_global_device_ids=true, to_apply=%region_14.15 | all-reduce | flops 1032 | bytes 8256 | tf_op jit(solution)/shard_map/psum | solution.py:75
  89.8 0.6 broadcast_in_dim.27
  90.4 1.1 %copy.31 = f32[128,3,512]{2,0,1:T(8,128)} copy(f32[128,3,512]{0,2,1:T(8,128)S(1)} %bitcast.25) | data formatting | bytes 1572864
  (10 shorter events, 0.2 us)
Async XLA Ops:
  4.4 21.4 %all-to-all-start = ((f32[64,1,2]{2,1,0:T(1,128)}), f32[64,1,2]{2,1,0:T(1,128)S(1)}, u32[]{:S(2)}, u32[]{:S(2)}) async-start(f32[64,1,2]{2,1,0:T(1,128)} %bitcast.4), calls=%async_computation | async-start | bytes 65536 | tf_op jit(solution)/shard_map/all_to_all | solution.py:56
  20.9 11.8 %copy-start = (f32[128,3,512]{2,0,1:T(8,128)S(1)}, f32[128,3,512]{2,0,1:T(8,128)}, u32[]{:S(2)}) copy-start(f32[128,3,512]{2,0,1:T(8,128)} %param.5) | copy-start | bytes 2359300
  25.8 30.0 %all-to-all-start.1 = ((f32[64,2,1536]{2,1,0:T(2,128)}), f32[64,2,1536]{2,1,0:T(2,128)S(1)}, u32[]{:S(2)}, u32[]{:S(2)}) async-start(f32[64,2,1536]{2,1,0:T(2,128)} %reshape.74), calls=%async_computation.1 | async-start | bytes 1572864 | tf_op jit(solution)/shard_map/all_to_all | solution.py:49
  32.6 1.0 %copy-start.1 = (s32[128,512]{1,0:T(8,128)S(1)}, s32[128,512]{1,0:T(8,128)}, u32[]{:S(2)}) copy-start(s32[128,512]{1,0:T(8,128)} %param.9) | copy-start | bytes 786436
where the time goes:
time: 91.9 us; the launch traced here: 91.5 us
  blocking collectives  30.6 us (33%)
  waiting for transfers between devices  24.4 us (27%)
  starting transfers between devices  20.4 us (22%)
  local copies, waits for them, and re-layouts  10 us (11%)
  other arithmetic  5.21 us (6%)
    psum x1, blocking collectives, shards(): sum_y, sum_z = lax.psum((part_y, part_z), 'sig')  30.6 us
    all_to_all x1, waiting for transfers between devices, shards(): lax.all_to_all(send_data.reshape(blocks, capacity, width), 'blk', split_a...  20.8 us
    all_to_all x1, starting transfers between devices, shards(): lax.all_to_all(send_tiles.reshape(blocks, capacity), 'blk', split_axis=0,...  13.6 us
    all_to_all x1, starting transfers between devices, shards(): lax.all_to_all(send_data.reshape(blocks, capacity, width), 'blk', split_a...  6.83 us
    all_to_all x1, waiting for transfers between devices, shards(): lax.all_to_all(send_tiles.reshape(blocks, capacity), 'blk', split_axis=0,...  3.56 us
    unnamed x8, local copies, waits for them, and re-layouts  2 us
    reduce_sum x1, other arithmetic, shards(): child_mean = 0.125 * jnp.sum(fine_fields, axis=2)  1.86 us
  transfers between devices with their start and end apart: 2, of which 2 were waited for; matrix products, arithmetic and copies ran while one was open for 7% of the time, Pallas kernels for 0%

commit v1 on v0

v1 whole, which is shorter than its diff:
```python
import jax
import jax.numpy as jnp
from jax import lax
from jax.experimental import pallas as pl
from jax.experimental.pallas import tpu as pltpu
from jax.sharding import PartitionSpec as P

EDGE = 8
CAP = 2
LANES = 128
CHUNKS = 4


def pack_kernel(owner, target, fine, out, buf, count, sems):
    patches, fields, children, cells = fine.shape
    chunk = patches // CHUNKS
    per_field = cells // LANES
    block = out.shape[0] // count.shape[0]
    tag_row = CAP * fields * per_field

    def fetch(k):
        part = pl.ds(k * chunk, chunk)
        return pltpu.make_async_copy(fine.at[part], buf.at[part], sems.at[k])

    for k in range(CHUNKS):
        fetch(k).start()
    lane = lax.broadcasted_iota(jnp.int32, (1, LANES), 1)
    zero_row = jnp.zeros((1, LANES), jnp.float32)
    for o in range(count.shape[0]):
        count[o] = 0
        out[o * block + tag_row] = zero_row
    first_row = []
    for i in range(patches):
        o = owner[i]
        rank = count[o]
        count[o] = rank + 1
        row = o * block + tag_row
        mark = (target[i] + 1).astype(jnp.float32)
        out[row] = jnp.where(lane == rank, mark, out[row])
        first_row.append(o * block + rank * (fields * per_field))
    for k in range(CHUNKS):
        fetch(k).wait()
        for i in range(k * chunk, (k + 1) * chunk):
            for f in range(fields):
                mean = 0.125 * jnp.sum(buf[i, f], axis=0, keepdims=True)
                for c in range(per_field):
                    out[first_row[i] + f * per_field + c] = mean[:, c * LANES : (c + 1) * LANES]


def pack(owner, target, fine, blocks):
    patches, fields, children, cells = fine.shape
    block = CAP * fields * cells // LANES + 1
    return pl.pallas_call(
        pack_kernel,
        out_shape=jax.ShapeDtypeStruct((blocks * block, 1, LANES), jnp.float32),
        in_specs=[
            pl.BlockSpec(memory_space=pltpu.SMEM),
            pl.BlockSpec(memory_space=pltpu.SMEM),
            pl.BlockSpec(memory_space=pl.ANY),
        ],
        out_specs=pl.BlockSpec(memory_space=pltpu.VMEM),
        scratch_shapes=[
            pltpu.VMEM(fine.shape, jnp.float32),
            pltpu.SMEM((blocks,), jnp.int32),
            pltpu.SemaphoreType.DMA((CHUNKS,)),
        ],
        compiler_params=pltpu.CompilerParams(vmem_limit_bytes=16 * 2**20),
        name="pack_patches",
    )(owner, target, fine)


def tile_kernel(got, coarse, tags, synced, parts, field_buf, marks, marks_f, weight_buf, sem):
    fields, tiles, cells = coarse.shape
    per_field = cells // LANES
    slot_rows = fields * per_field
    block = CAP * slot_rows + 1
    blocks = got.shape[0] // block
    copies, part_rows = parts.shape[0], parts.shape[1]
    y_rows = part_rows - 1

    for b in range(blocks):
        marks[b] = got[b * block + CAP * slot_rows]
    to_scalar = pltpu.make_async_copy(marks, marks_f, sem)
    to_scalar.start()
    for f in range(fields):
        for c in range(per_field):
            field_buf[f * per_field + c, :tiles] = coarse[f, :, c * LANES : (c + 1) * LANES]
    to_scalar.wait()
    for b in range(blocks):
        for r in range(CAP):
            mark = marks_f[b, 0, r].astype(jnp.int32)
            tile = jnp.where(mark > 0, mark - 1, tiles)
            base = b * block + r * slot_rows
            for j in range(slot_rows):
                field_buf[j, pl.ds(tile, 1)] = got[base + j]

    lane = lax.broadcasted_iota(jnp.int32, (EDGE, LANES), 1)
    z = lane % EDGE
    y = (lane // EDGE) % EDGE
    upper = lane >= EDGE * EDGE
    inner_z = (z > 0) & (z < EDGE - 1)
    inner_y = (y > 0) & (y < EDGE - 1)
    total = jnp.zeros((EDGE, LANES), jnp.float32)
    for g in range(tiles // 8):
        rows = pl.ds(g * 8, 8)
        sum_z = [None] * per_field
        sum_y = [None] * per_field
        sum_x = [None] * (per_field - 1)
        for f in range(fields):
            v = [field_buf[f * per_field + c, rows] for c in range(per_field)]
            for c in range(per_field):
                synced[f, rows, c * LANES : (c + 1) * LANES] = v[c]
                dz = v[c] - pltpu.roll(v[c], 2, 1)
                dy = v[c] - pltpu.roll(v[c], 2 * EDGE, 1)
                sum_z[c] = dz * dz if f == 0 else sum_z[c] + dz * dz
                sum_y[c] = dy * dy if f == 0 else sum_y[c] + dy * dy
                if c:
                    dx = v[c] - v[c - 1]
                    sum_x[c - 1] = dx * dx if f == 0 else sum_x[c - 1] + dx * dx
        turned = [pltpu.roll(s, EDGE * EDGE, 1) for s in sum_x]
        weight = None
        for c in range(per_field):
            along_z = jnp.where(inner_z, pltpu.roll(sum_z[c], LANES - 1, 1), 0.0)
            along_y = jnp.where(inner_y, pltpu.roll(sum_y[c], LANES - EDGE, 1), 0.0)
            above = turned[c] if c < per_field - 1 else jnp.zeros_like(along_z)
            below = turned[c - 1] if c else jnp.zeros_like(along_z)
            along_x = jnp.where(upper, above, below)
            tag = tags[rows, c * LANES : (c + 1) * LANES].astype(jnp.float32)
            term = tag * (along_x + along_y + along_z)
            weight = term if c == 0 else weight + term
        weight_buf[rows] = weight
        total = total + weight
    weight_buf[pl.ds(tiles, 8)] = total

    src = lax.broadcasted_iota(jnp.int32, (LANES, LANES), 0)
    dst = lax.broadcasted_iota(jnp.int32, (LANES, LANES), 1)
    pick_y = ((src // EDGE) % EDGE == dst % EDGE).astype(jnp.float32)
    pick_z = (src % EDGE == dst).astype(jnp.float32)
    high = lax.Precision.HIGHEST
    by_y = jnp.dot(
        weight_buf[:tiles], pick_y, precision=high, preferred_element_type=jnp.float32
    )
    by_z = jnp.dot(
        weight_buf[pl.ds(tiles, 8)], pick_z, precision=high, preferred_element_type=jnp.float32
    )
    per_row = LANES // EDGE
    row_tile = lax.broadcasted_iota(jnp.int32, (per_row, LANES), 0)
    row_lane = lax.broadcasted_iota(jnp.int32, (per_row, LANES), 1)
    own = row_lane // EDGE == row_tile
    for r in range(y_rows):
        piece = jnp.where(own, by_y[r * per_row : (r + 1) * per_row], 0.0)
        line = 0.25 * jnp.sum(piece, axis=0, keepdims=True)
        for k in range(copies):
            parts[k, r] = line
    line = 0.25 * jnp.sum(by_z, axis=0, keepdims=True)
    for k in range(copies):
        parts[k, y_rows] = line


def tile_step(got, coarse, tags, slabs):
    fields, tiles, cells = coarse.shape
    block = CAP * fields * cells // LANES + 1
    blocks = got.shape[0] // block
    part_rows = tiles * EDGE // LANES + 1
    vmem = pl.BlockSpec(memory_space=pltpu.VMEM)
    return pl.pallas_call(
        tile_kernel,
        out_shape=(
            jax.ShapeDtypeStruct(coarse.shape, jnp.float32),
            jax.ShapeDtypeStruct((slabs, part_rows, 1, LANES), jnp.float32),
        ),
        in_specs=[vmem, vmem, vmem],
        out_specs=(vmem, vmem),
        scratch_shapes=[
            pltpu.VMEM((fields * cells // LANES, tiles + 8, LANES), jnp.float32),
            pltpu.VMEM((blocks, 1, LANES), jnp.float32),
            pltpu.SMEM((blocks, 1, LANES), jnp.float32),
            pltpu.VMEM((tiles + 8, LANES), jnp.float32),
            pltpu.SemaphoreType.DMA,
        ],
        compiler_params=pltpu.CompilerParams(vmem_limit_bytes=16 * 2**20),
        name="tile_step",
    )(got, coarse, tags)


def sum_kernel(along_y_cells, along_z_cells, parts, out):
    y_rows = parts.shape[1] - 1
    for r in range(y_rows + 1):
        line = parts[0, r]
        for k in range(1, parts.shape[0]):
            line = line + parts[k, r]
        if r < y_rows:
            out[:, r * LANES : (r + 1) * LANES] = line * (1.0 / along_y_cells)
        else:
            out[:, r * LANES :] = line[:, :EDGE] * (1.0 / along_z_cells)


def sum_parts(parts, tiles, slabs):
    width = tiles * EDGE + EDGE
    along_y_cells = EDGE * EDGE * slabs
    along_z_cells = EDGE * EDGE * tiles * slabs
    return pl.pallas_call(
        lambda p, o: sum_kernel(along_y_cells, along_z_cells, p, o),
        out_shape=jax.ShapeDtypeStruct((1, width), jnp.float32),
        in_specs=[pl.BlockSpec(memory_space=pltpu.VMEM)],
        out_specs=pl.BlockSpec(memory_space=pltpu.VMEM),
        name="sum_parts",
    )(parts)


def shards(coarse_fields, fine_fields, owner, target_tile, tags):
    tiles = coarse_fields.shape[0]
    blocks = lax.axis_size("blk")
    slabs = lax.axis_size("sig")
    sent = pack(owner[:, 0], target_tile[:, 0], fine_fields, blocks)
    rows = sent.shape[0] // blocks
    got = lax.all_to_all(
        sent.reshape(blocks, rows, 1, LANES), "blk", split_axis=0, concat_axis=0, tiled=True
    )
    got = got.reshape(blocks * rows, 1, LANES)
    coarse = jnp.transpose(coarse_fields, (1, 0, 2))
    synced, parts = tile_step(got, coarse, tags, slabs)
    parts = lax.all_to_all(parts, "sig", split_axis=0, concat_axis=0, tiled=True)
    signature = sum_parts(parts, tiles, slabs)
    return (jnp.transpose(synced, (1, 0, 2)), signature)


def solution(mesh):
    return jax.shard_map(
        shards,
        mesh=mesh,
        in_specs=(
            P(("blk", "sig"), None, None),
            P(("blk", "sig"), None, None, None),
            P(("blk", "sig"), None),
            P(("blk", "sig"), None),
            P(("blk", "sig"), None),
        ),
        out_specs=(P(("blk", "sig"), None, None), P("blk", None)),
        check_vma=False,
    )
```

time: 91.9 us -> 70.8 us (0.77)
  the two profiles are of different devices: /device:TPU:4 before, /device:TPU:2 now
where the time goes in v1:
time: 70.8 us; the launch traced here: 70.5 us
  blocking collectives  60.3 us (85%)
  Pallas kernels  6.83 us (10%)
  local copies, waits for them, and re-layouts  2.72 us (4%)
    all_to_all x1, blocking collectives, shards(): lax.all_to_all(sent.reshape(blocks, rows, 1, LANES), 'blk', split_axis=0,...  36.8 us
    all_to_all x1, blocking collectives, shards(): lax.all_to_all(parts, 'sig', split_axis=0, concat_axis=0, tiled=True)  23.5 us
    pallas_call x1, Pallas kernels, tile_step(): pl.pallas_call(tile_kernel, out_shape=(jax.ShapeDtypeStruct(coarse.shape,...  3.51 us
    unnamed x10, local copies, waits for them, and re-layouts  2.72 us
    pallas_call x1, Pallas kernels, pack(): pl.pallas_call(pack_kernel, out_shape=jax.ShapeDtypeStruct((blocks * bloc...  1.89 us
    pallas_call x1, Pallas kernels, sum_parts(): pl.pallas_call(lambda p, o: sum_kernel(along_y_cells, along_z_cells, p, o...  1.43 us

profile of v1, /device:TPU:2, one launch (start us, length us, event | category | flops | bytes accessed | tf_op | source)
XLA Modules:
  0.0 70.5 jit_solution(1907135254963380680)
XLA Ops:
  0.6 0.0 copy-start
  0.6 1.4 %copy-done = f32[32,3,8,512]{3,2,1,0:T(8,128)S(1)} copy-done((f32[32,3,8,512]{3,2,1,0:T(8,128)S(1)}, f32[32,3,8,512]{3,2,1,0:T(8,128)}, u32[]{:S(2)}) %copy-start) | copy-done | bytes 1572888
  2.0 0.0 copy-start.3
  2.0 0.7 copy-done.3
  2.7 0.0 copy-start.4
  2.7 0.7 copy-done.4
  3.4 0.0 copy-start.1
  3.4 0.0 copy-start.2
  3.4 1.9 %pack_patches.1 = f32[1600,1,128]{2,1,0:T(1,128)S(1)} custom-call(s32[32]{0:T(128)S(1)} %bitcast.9, s32[32]{0:T(128)S(1)} %bitcast.10, f32[32,3,8,512]{3,2,1,0:T(8,128)S(1)} %copy-done), custom_call_target="tpu_custom_call" | custom-call | tf_op jit(solution)/shard_map/pack_patches/pallas_call | solution.py:53
  5.2 36.8 %all_to_all.10 = f32[64,25,1,128]{3,2,1,0:T(1,128)S(1)} all-to-all(f32[64,25,1,128]{3,2,1,0:T(1,128)S(1)} %bitcast.7), channel_id=1, replica_groups=mesh['blk'=64,'sig'=12] {'blk'}, dimensions={0} | all-to-all | bytes 1638400 | tf_op jit(solution)/shard_map/all_to_all | solution.py:217
  42.0 0.0 copy-done.1
  42.0 0.0 copy-done.2
  42.0 3.5 %tile_step.1 = (f32[3,128,512]{2,1,0:T(8,128)}, f32[12,9,1,128]{3,2,1,0:T(1,128)S(1)}) custom-call(f32[1600,1,128]{2,1,0:T(1,128)S(1)} %bitcast.6, f32[3,128,512]{2,1,0:T(8,128)S(1)} %bitcast.8, s32[128,512]{1,0:T(8,128)S(1)} %copy-done.2), custom_call_target="tpu_custom_call" | custom-call | tf_op jit(solution)/shard_map/tile_step/pallas_call | solution.py:166
  45.6 23.5 %all_to_all.11.p = f32[12,9,1,128]{3,2,1,0:T(1,128)} all-to-all(f32[12,9,1,128]{3,2,1,0:T(1,128)S(1)} %get-tuple-element.5), channel_id=1, replica_groups=mesh['blk'=64,'sig'=12] {'sig'}, dimensions={0} | all-to-all | bytes 110592 | tf_op jit(solution)/shard_map/all_to_all | solution.py:223
  69.1 1.4 %sum_parts.1 = f32[1,1032]{1,0:T(1,128)} custom-call(f32[12,9,1,128]{3,2,1,0:T(1,128)} %all_to_all.11.p), custom_call_target="tpu_custom_call" | custom-call | tf_op jit(solution)/shard_map/sum_parts/pallas_call | solution.py:202
Async XLA Ops:
  0.6 1.4 %copy-start = (f32[32,3,8,512]{3,2,1,0:T(8,128)S(1)}, f32[32,3,8,512]{3,2,1,0:T(8,128)}, u32[]{:S(2)}) copy-start(f32[32,3,8,512]{3,2,1,0:T(8,128)} %fine.1) | copy-start | bytes 4718596
  2.0 0.7 copy-start.3
  2.7 0.7 copy-start.4
  3.4 38.7 %copy-start.1 = (f32[128,3,512]{2,0,1:T(8,128)S(1)}, f32[128,3,512]{2,0,1:T(8,128)}, u32[]{:S(2)}) copy-start(f32[128,3,512]{2,0,1:T(8,128)} %param.5) | copy-start | bytes 2359300
  3.4 38.7 %copy-start.2 = (s32[128,512]{1,0:T(8,128)S(1)}, s32[128,512]{1,0:T(8,128)}, u32[]{:S(2)}) copy-start(s32[128,512]{1,0:T(8,128)} %tags.1) | copy-start | bytes 786436

commit v2 on v1

--- a/solution.py
+++ b/solution.py
@@ -11,88 +11,128 @@
 CHUNKS = 4
 
 
-def pack_kernel(owner, target, fine, out, buf, count, sems):
+def pack_kernel(owner, target, fine, out, buf, means, marks, owner_s, target_s, count, sems):
     patches, fields, children, cells = fine.shape
     chunk = patches // CHUNKS
     per_field = cells // LANES
-    block = out.shape[0] // count.shape[0]
-    tag_row = CAP * fields * per_field
+    slot_rows = fields * per_field
+    blocks = out.shape[0]
 
     def fetch(k):
         part = pl.ds(k * chunk, chunk)
         return pltpu.make_async_copy(fine.at[part], buf.at[part], sems.at[k])
 
+    owner_copy = pltpu.make_async_copy(owner, owner_s, sems.at[CHUNKS])
+    target_copy = pltpu.make_async_copy(target, target_s, sems.at[CHUNKS + 1])
+    owner_copy.start()
+    target_copy.start()
     for k in range(CHUNKS):
         fetch(k).start()
     lane = lax.broadcasted_iota(jnp.int32, (1, LANES), 1)
-    zero_row = jnp.zeros((1, LANES), jnp.float32)
-    for o in range(count.shape[0]):
+    own_lane = CAP * lax.axis_index("blk")
+    for o in range(blocks):
         count[o] = 0
-        out[o * block + tag_row] = zero_row
-    first_row = []
+        marks[o] = jnp.zeros((1, LANES), jnp.float32)
+    owner_copy.wait()
+    target_copy.wait()
+    slots = []
     for i in range(patches):
-        o = owner[i]
+        o = owner_s[i]
         rank = count[o]
         count[o] = rank + 1
-        row = o * block + tag_row
-        mark = (target[i] + 1).astype(jnp.float32)
-        out[row] = jnp.where(lane == rank, mark, out[row])
-        first_row.append(o * block + rank * (fields * per_field))
+        mark = (target_s[i] + 1).astype(jnp.float32)
+        marks[o] = jnp.where(lane == own_lane + rank, mark, marks[o])
+        slots.append((o, rank))
+    leave_marks = pltpu.make_async_copy(marks, out.at[:, CAP * slot_rows], sems.at[CHUNKS + 2])
+    leave_marks.start()
+
+    def leave(i):
+        o, rank = slots[i]
+        return pltpu.make_async_copy(
+            means.at[pl.ds(i * slot_rows, slot_rows)],
+            out.at[o, pl.ds(rank * slot_rows, slot_rows)],
+            sems.at[CHUNKS + 3 + i],
+        )
+
     for k in range(CHUNKS):
         fetch(k).wait()
         for i in range(k * chunk, (k + 1) * chunk):
             for f in range(fields):
                 mean = 0.125 * jnp.sum(buf[i, f], axis=0, keepdims=True)
                 for c in range(per_field):
-                    out[first_row[i] + f * per_field + c] = mean[:, c * LANES : (c + 1) * LANES]
+                    means[i * slot_rows + f * per_field + c] = mean[:, c * LANES : (c + 1) * LANES]
+            leave(i).start()
+    leave_marks.wait()
+    for i in range(patches):
+        leave(i).wait()
 
 
 def pack(owner, target, fine, blocks):
     patches, fields, children, cells = fine.shape
-    block = CAP * fields * cells // LANES + 1
+    slot_rows = fields * cells // LANES
+    hbm = pl.BlockSpec(memory_space=pltpu.HBM)
     return pl.pallas_call(
         pack_kernel,
-        out_shape=jax.ShapeDtypeStruct((blocks * block, 1, LANES), jnp.float32),
-        in_specs=[
-            pl.BlockSpec(memory_space=pltpu.SMEM),
-            pl.BlockSpec(memory_space=pltpu.SMEM),
-            pl.BlockSpec(memory_space=pl.ANY),
-        ],
-        out_specs=pl.BlockSpec(memory_space=pltpu.VMEM),
+        out_shape=jax.ShapeDtypeStruct((blocks, CAP * slot_rows + 1, 1, LANES), jnp.float32),
+        in_specs=[hbm, hbm, hbm],
+        out_specs=hbm,
         scratch_shapes=[
             pltpu.VMEM(fine.shape, jnp.float32),
+            pltpu.VMEM((patches * slot_rows, 1, LANES), jnp.float32),
+            pltpu.VMEM((blocks, 1, LANES), jnp.float32),
+            pltpu.SMEM((patches,), jnp.int32),
+            pltpu.SMEM((patches,), jnp.int32),
             pltpu.SMEM((blocks,), jnp.int32),
-            pltpu.SemaphoreType.DMA((CHUNKS,)),
+            pltpu.SemaphoreType.DMA((CHUNKS + 3 + patches,)),
         ],
-        compiler_params=pltpu.CompilerParams(vmem_limit_bytes=16 * 2**20),
+        compiler_params=pltpu.CompilerParams(vmem_limit_bytes=60 * 2**20),
         name="pack_patches",
     )(owner, target, fine)
 
 
-def tile_kernel(got, coarse, tags, synced, parts, field_buf, marks, marks_f, weight_buf, sem):
+def tile_kernel(got, coarse, tags, synced, parts, fields_v, marks_v, marks_s, weight_v, sems):
     fields, tiles, cells = coarse.shape
     per_field = cells // LANES
     slot_rows = fields * per_field
     block = CAP * slot_rows + 1
     blocks = got.shape[0] // block
+    pitch = tiles + 8
     copies, part_rows = parts.shape[0], parts.shape[1]
     y_rows = part_rows - 1
 
+    marks = [None] * 4
     for b in range(blocks):
-        marks[b] = got[b * block + CAP * slot_rows]
-    to_scalar = pltpu.make_async_copy(marks, marks_f, sem)
+        row = got[pl.ds(b * block + CAP * slot_rows, 1)]
+        marks[b % 4] = row if b < 4 else marks[b % 4] + row
+    mark = ((marks[0] + marks[1]) + (marks[2] + marks[3])).astype(jnp.int32)
+    marks_v[...] = jnp.where(mark > 0, mark - 1, tiles)
+    to_scalar = pltpu.make_async_copy(marks_v, marks_s, sems.at[slot_rows])
     to_scalar.start()
     for f in range(fields):
         for c in range(per_field):
-            field_buf[f * per_field + c, :tiles] = coarse[f, :, c * LANES : (c + 1) * LANES]
+            fields_v[pl.ds((f * per_field + c) * pitch, tiles)] = coarse[
+                f, :, c * LANES : (c + 1) * LANES
+            ]
     to_scalar.wait()
     for b in range(blocks):
         for r in range(CAP):
-            mark = marks_f[b, 0, r].astype(jnp.int32)
-            tile = jnp.where(mark > 0, mark - 1, tiles)
+            tile = marks_s[0, CAP * b + r]
             base = b * block + r * slot_rows
-            for j in range(slot_rows):
-                field_buf[j, pl.ds(tile, 1)] = got[base + j]
+            for j in range(0, slot_rows, 8):
+                n = min(8, slot_rows - j)
+                fields_v[pl.ds(tile + j * pitch, n, stride=pitch)] = got[base + j : base + j + n]
+
+    def leave(f, c):
+        j = f * per_field + c
+        return pltpu.make_async_copy(
+            fields_v.at[pl.ds(j * pitch, tiles)],
+            synced.at[f, :, pl.ds(c * LANES, LANES)],
+            sems.at[j],
+        )
+
+    for f in range(fields):
+        for c in range(per_field):
+            leave(f, c).start()
 
     lane = lax.broadcasted_iota(jnp.int32, (EDGE, LANES), 1)
     z = lane % EDGE
@@ -107,9 +147,8 @@
         sum_y = [None] * per_field
         sum_x = [None] * (per_field - 1)
         for f in range(fields):
-            v = [field_buf[f * per_field + c, rows] for c in range(per_field)]
+            v = [fields_v[pl.ds((f * per_field + c) * pitch + g * 8, 8)] for c in range(per_field)]
             for c in range(per_field):
-                synced[f, rows, c * LANES : (c + 1) * LANES] = v[c]
                 dz = v[c] - pltpu.roll(v[c], 2, 1)
                 dy = v[c] - pltpu.roll(v[c], 2 * EDGE, 1)
                 sum_z[c] = dz * dz if f == 0 else sum_z[c] + dz * dz
@@ -128,20 +167,18 @@
             tag = tags[rows, c * LANES : (c + 1) * LANES].astype(jnp.float32)
             term = tag * (along_x + along_y + along_z)
             weight = term if c == 0 else weight + term
-        weight_buf[rows] = weight
+        weight_v[rows] = weight
         total = total + weight
-    weight_buf[pl.ds(tiles, 8)] = total
+    weight_v[pl.ds(tiles, 8)] = total
 
     src = lax.broadcasted_iota(jnp.int32, (LANES, LANES), 0)
     dst = lax.broadcasted_iota(jnp.int32, (LANES, LANES), 1)
     pick_y = ((src // EDGE) % EDGE == dst % EDGE).astype(jnp.float32)
     pick_z = (src % EDGE == dst).astype(jnp.float32)
     high = lax.Precision.HIGHEST
-    by_y = jnp.dot(
-        weight_buf[:tiles], pick_y, precision=high, preferred_element_type=jnp.float32
-    )
+    by_y = jnp.dot(weight_v[:tiles], pick_y, precision=high, preferred_element_type=jnp.float32)
     by_z = jnp.dot(
-        weight_buf[pl.ds(tiles, 8)], pick_z, precision=high, preferred_element_type=jnp.float32
+        weight_v[pl.ds(tiles, 8)], pick_z, precision=high, preferred_element_type=jnp.float32
     )
     per_row = LANES // EDGE
     row_tile = lax.broadcasted_iota(jnp.int32, (per_row, LANES), 0)
@@ -155,12 +192,15 @@
     line = 0.25 * jnp.sum(by_z, axis=0, keepdims=True)
     for k in range(copies):
         parts[k, y_rows] = line
+    for f in range(fields):
+        for c in range(per_field):
+            leave(f, c).wait()
 
 
 def tile_step(got, coarse, tags, slabs):
     fields, tiles, cells = coarse.shape
-    block = CAP * fields * cells // LANES + 1
-    blocks = got.shape[0] // block
+    slot_rows = fields * cells // LANES
+    blocks = got.shape[0] // (CAP * slot_rows + 1)
     part_rows = tiles * EDGE // LANES + 1
     vmem = pl.BlockSpec(memory_space=pltpu.VMEM)
     return pl.pallas_call(
@@ -170,13 +210,13 @@
             jax.ShapeDtypeStruct((slabs, part_rows, 1, LANES), jnp.float32),
         ),
         in_specs=[vmem, vmem, vmem],
-        out_specs=(vmem, vmem),
+        out_specs=(pl.BlockSpec(memory_space=pltpu.HBM), vmem),
         scratch_shapes=[
-            pltpu.VMEM((fields * cells // LANES, tiles + 8, LANES), jnp.float32),
-            pltpu.VMEM((blocks, 1, LANES), jnp.float32),
-            pltpu.SMEM((blocks, 1, LANES), jnp.float32),
+            pltpu.VMEM(((slot_rows + 1) * (tiles + 8), LANES), jnp.float32),
+            pltpu.VMEM((1, LANES), jnp.int32),
+            pltpu.SMEM((1, LANES), jnp.int32),
             pltpu.VMEM((tiles + 8, LANES), jnp.float32),
-            pltpu.SemaphoreType.DMA,
+            pltpu.SemaphoreType.DMA((slot_rows + 1,)),
         ],
         compiler_params=pltpu.CompilerParams(vmem_limit_bytes=16 * 2**20),
         name="tile_step",
@@ -213,11 +253,8 @@
     blocks = lax.axis_size("blk")
     slabs = lax.axis_size("sig")
     sent = pack(owner[:, 0], target_tile[:, 0], fine_fields, blocks)
-    rows = sent.shape[0] // blocks
-    got = lax.all_to_all(
-        sent.reshape(blocks, rows, 1, LANES), "blk", split_axis=0, concat_axis=0, tiled=True
-    )
-    got = got.reshape(blocks * rows, 1, LANES)
+    got = lax.all_to_all(sent, "blk", split_axis=0, concat_axis=0, tiled=True)
+    got = got.reshape(-1, LANES)
     coarse = jnp.transpose(coarse_fields, (1, 0, 2))
     synced, parts = tile_step(got, coarse, tags, slabs)
     parts = lax.all_to_all(parts, "sig", split_axis=0, concat_axis=0, tiled=True)

time: 70.8 us -> 68.1 us (0.962)
  local copies, waits for them, and re-layouts: 2.72 us -> 0.01 us
    unnamed x10 -> x4, local copies, waits for them, and re-layouts: 2.72 us -> 0.01 us
    all_to_all x1, blocking collectives: 36.8 us -> 37.7 us  [shards(): got = lax.all_to_all(sent, 'blk', split_axis=0, concat_axis=0, tiled=True)]
    pallas_call x1, Pallas kernels: 3.51 us -> 2.67 us  [tile_step(): pl.pallas_call(tile_kernel, out_shape=(jax.ShapeDtypeStruct(coarse.shape,...]
where the time goes in v2:
time: 68.1 us; the launch traced here: 67.8 us
  blocking collectives  60.6 us (89%)
  Pallas kernels  6.57 us (10%)
    all_to_all x1, blocking collectives, shards(): got = lax.all_to_all(sent, 'blk', split_axis=0, concat_axis=0, tiled=True)  37.7 us
    all_to_all x1, blocking collectives, shards(): lax.all_to_all(parts, 'sig', split_axis=0, concat_axis=0, tiled=True)  22.9 us
    pallas_call x1, Pallas kernels, tile_step(): pl.pallas_call(tile_kernel, out_shape=(jax.ShapeDtypeStruct(coarse.shape,...  2.67 us
    pallas_call x1, Pallas kernels, pack(): pl.pallas_call(pack_kernel, out_shape=jax.ShapeDtypeStruct((blocks, CAP *...  2.47 us
    pallas_call x1, Pallas kernels, sum_parts(): pl.pallas_call(lambda p, o: sum_kernel(along_y_cells, along_z_cells, p, o...  1.43 us

profile of v2, /device:TPU:2, one launch (start us, length us, event | category | flops | bytes accessed | tf_op | source)
XLA Modules:
  0.0 67.8 jit_solution(17957809454886732696)
XLA Ops:
  0.6 0.0 copy-start
  0.6 0.0 copy-start.1
  0.7 2.5 %pack_patches.1 = f32[64,25,1,128]{3,2,1,0:T(1,128)} custom-call(s32[32]{0:T(128)} %bitcast.7, s32[32]{0:T(128)} %bitcast.8, f32[32,3,8,512]{3,2,1,0:T(8,128)} %fine.1), custom_call_target="tpu_custom_call" | custom-call | tf_op jit(solution)/shard_map/pack_patches/pallas_call | solution.py:74
  3.1 37.7 %all_to_all.10 = f32[64,25,1,128]{3,2,1,0:T(1,128)S(1)} all-to-all(f32[64,25,1,128]{3,2,1,0:T(1,128)} %pack_patches.1), channel_id=1, replica_groups=mesh['blk'=64,'sig'=12] {'blk'}, dimensions={0} | all-to-all | bytes 1638400 | tf_op jit(solution)/shard_map/all_to_all | solution.py:256
  40.8 0.0 copy-done
  40.8 0.0 copy-done.1
  40.8 2.7 %tile_step.1 = (f32[3,128,512]{2,1,0:T(8,128)}, f32[12,9,1,128]{3,2,1,0:T(1,128)S(1)}) custom-call(f32[1600,128]{1,0:T(8,128)S(1)} %bitcast.5, f32[3,128,512]{2,1,0:T(8,128)S(1)} %bitcast.6, s32[128,512]{1,0:T(8,128)S(1)} %copy-done.1), custom_call_target="tpu_custom_call" | custom-call | tf_op jit(solution)/shard_map/tile_step/pallas_call | solution.py:206
  43.5 22.9 %all_to_all.11.p = f32[12,9,1,128]{3,2,1,0:T(1,128)} all-to-all(f32[12,9,1,128]{3,2,1,0:T(1,128)S(1)} %get-tuple-element.5), channel_id=1, replica_groups=mesh['blk'=64,'sig'=12] {'sig'}, dimensions={0} | all-to-all | bytes 110592 | tf_op jit(solution)/shard_map/all_to_all | solution.py:260
  66.4 1.4 %sum_parts.1 = f32[1,1032]{1,0:T(1,128)} custom-call(f32[12,9,1,128]{3,2,1,0:T(1,128)} %all_to_all.11.p), custom_call_target="tpu_custom_call" | custom-call | tf_op jit(solution)/shard_map/sum_parts/pallas_call | solution.py:242
Async XLA Ops:
  0.6 40.2 %copy-start = (f32[128,3,512]{2,0,1:T(8,128)S(1)}, f32[128,3,512]{2,0,1:T(8,128)}, u32[]{:S(2)}) copy-start(f32[128,3,512]{2,0,1:T(8,128)} %param.5) | copy-start | bytes 2359300
  0.6 40.2 %copy-start.1 = (s32[128,512]{1,0:T(8,128)S(1)}, s32[128,512]{1,0:T(8,128)}, u32[]{:S(2)}) copy-start(s32[128,512]{1,0:T(8,128)} %tags.1) | copy-start | bytes 786436

commit v3 on v2

--- a/solution.py
+++ b/solution.py
@@ -1,3 +1,5 @@
+import functools
+
 import jax
 import jax.numpy as jnp
 from jax import lax
@@ -8,25 +10,27 @@
 EDGE = 8
 CAP = 2
 LANES = 128
-CHUNKS = 4
+CHUNKS = (3, 3, 1, 1)
 
 
 def pack_kernel(owner, target, fine, out, buf, means, marks, owner_s, target_s, count, sems):
     patches, fields, children, cells = fine.shape
-    chunk = patches // CHUNKS
+    chunk = patches // sum(CHUNKS)
+    ends = [chunk * sum(CHUNKS[: k + 1]) for k in range(len(CHUNKS))]
+    starts = [0] + ends[:-1]
     per_field = cells // LANES
     slot_rows = fields * per_field
     blocks = out.shape[0]
 
     def fetch(k):
-        part = pl.ds(k * chunk, chunk)
+        part = pl.ds(starts[k], ends[k] - starts[k])
         return pltpu.make_async_copy(fine.at[part], buf.at[part], sems.at[k])
 
-    owner_copy = pltpu.make_async_copy(owner, owner_s, sems.at[CHUNKS])
-    target_copy = pltpu.make_async_copy(target, target_s, sems.at[CHUNKS + 1])
+    owner_copy = pltpu.make_async_copy(owner, owner_s, sems.at[len(CHUNKS)])
+    target_copy = pltpu.make_async_copy(target, target_s, sems.at[len(CHUNKS) + 1])
     owner_copy.start()
     target_copy.start()
-    for k in range(CHUNKS):
+    for k in range(len(CHUNKS)):
         fetch(k).start()
     lane = lax.broadcasted_iota(jnp.int32, (1, LANES), 1)
     own_lane = CAP * lax.axis_index("blk")
@@ -43,7 +47,7 @@
         mark = (target_s[i] + 1).astype(jnp.float32)
         marks[o] = jnp.where(lane == own_lane + rank, mark, marks[o])
         slots.append((o, rank))
-    leave_marks = pltpu.make_async_copy(marks, out.at[:, CAP * slot_rows], sems.at[CHUNKS + 2])
+    leave_marks = pltpu.make_async_copy(marks, out.at[:, CAP * slot_rows], sems.at[len(CHUNKS) + 2])
     leave_marks.start()
 
     def leave(i):
@@ -51,12 +55,12 @@
         return pltpu.make_async_copy(
             means.at[pl.ds(i * slot_rows, slot_rows)],
             out.at[o, pl.ds(rank * slot_rows, slot_rows)],
-            sems.at[CHUNKS + 3 + i],
+            sems.at[len(CHUNKS) + 3 + i],
         )
 
-    for k in range(CHUNKS):
+    for k in range(len(CHUNKS)):
         fetch(k).wait()
-        for i in range(k * chunk, (k + 1) * chunk):
+        for i in range(starts[k], ends[k]):
             for f in range(fields):
                 mean = 0.125 * jnp.sum(buf[i, f], axis=0, keepdims=True)
                 for c in range(per_field):
@@ -83,14 +87,14 @@
             pltpu.SMEM((patches,), jnp.int32),
             pltpu.SMEM((patches,), jnp.int32),
             pltpu.SMEM((blocks,), jnp.int32),
-            pltpu.SemaphoreType.DMA((CHUNKS + 3 + patches,)),
+            pltpu.SemaphoreType.DMA((len(CHUNKS) + 3 + patches,)),
         ],
-        compiler_params=pltpu.CompilerParams(vmem_limit_bytes=60 * 2**20),
+        compiler_params=pltpu.CompilerParams(vmem_limit_bytes=64 * 2**20 - 2**17),
         name="pack_patches",
     )(owner, target, fine)
 
 
-def tile_kernel(got, coarse, tags, synced, parts, fields_v, marks_v, marks_s, weight_v, sems):
+def tile_kernel(got, coarse, tags, fields_v, parts, weight_v):
     fields, tiles, cells = coarse.shape
     per_field = cells // LANES
     slot_rows = fields * per_field
@@ -105,34 +109,19 @@
         row = got[pl.ds(b * block + CAP * slot_rows, 1)]
         marks[b % 4] = row if b < 4 else marks[b % 4] + row
     mark = ((marks[0] + marks[1]) + (marks[2] + marks[3])).astype(jnp.int32)
-    marks_v[...] = jnp.where(mark > 0, mark - 1, tiles)
-    to_scalar = pltpu.make_async_copy(marks_v, marks_s, sems.at[slot_rows])
-    to_scalar.start()
+    tile_of = jnp.where(mark > 0, mark - 1, tiles)
     for f in range(fields):
         for c in range(per_field):
             fields_v[pl.ds((f * per_field + c) * pitch, tiles)] = coarse[
                 f, :, c * LANES : (c + 1) * LANES
             ]
-    to_scalar.wait()
     for b in range(blocks):
         for r in range(CAP):
-            tile = marks_s[0, CAP * b + r]
+            tile = tile_of[0, CAP * b + r]
             base = b * block + r * slot_rows
             for j in range(0, slot_rows, 8):
                 n = min(8, slot_rows - j)
                 fields_v[pl.ds(tile + j * pitch, n, stride=pitch)] = got[base + j : base + j + n]
-
-    def leave(f, c):
-        j = f * per_field + c
-        return pltpu.make_async_copy(
-            fields_v.at[pl.ds(j * pitch, tiles)],
-            synced.at[f, :, pl.ds(c * LANES, LANES)],
-            sems.at[j],
-        )
-
-    for f in range(fields):
-        for c in range(per_field):
-            leave(f, c).start()
 
     lane = lax.broadcasted_iota(jnp.int32, (EDGE, LANES), 1)
     z = lane % EDGE
@@ -192,10 +181,6 @@
     line = 0.25 * jnp.sum(by_z, axis=0, keepdims=True)
     for k in range(copies):
         parts[k, y_rows] = line
-    for f in range(fields):
-        for c in range(per_field):
-            leave(f, c).wait()
-
 
 def tile_step(got, coarse, tags, slabs):
     fields, tiles, cells = coarse.shape
@@ -206,24 +191,33 @@
     return pl.pallas_call(
         tile_kernel,
         out_shape=(
-            jax.ShapeDtypeStruct(coarse.shape, jnp.float32),
+            jax.ShapeDtypeStruct(((slot_rows + 1) * (tiles + 8), LANES), jnp.float32),
             jax.ShapeDtypeStruct((slabs, part_rows, 1, LANES), jnp.float32),
         ),
         in_specs=[vmem, vmem, vmem],
-        out_specs=(pl.BlockSpec(memory_space=pltpu.HBM), vmem),
+        out_specs=(vmem, vmem),
         scratch_shapes=[
-            pltpu.VMEM(((slot_rows + 1) * (tiles + 8), LANES), jnp.float32),
-            pltpu.VMEM((1, LANES), jnp.int32),
-            pltpu.SMEM((1, LANES), jnp.int32),
             pltpu.VMEM((tiles + 8, LANES), jnp.float32),
-            pltpu.SemaphoreType.DMA((slot_rows + 1,)),
         ],
         compiler_params=pltpu.CompilerParams(vmem_limit_bytes=16 * 2**20),
         name="tile_step",
     )(got, coarse, tags)
 
 
-def sum_kernel(along_y_cells, along_z_cells, parts, out):
+def finish_kernel(along_y_cells, along_z_cells, fields_v, parts, synced, out, sems):
+    fields, tiles, cells = synced.shape
+    per_field = cells // LANES
+    copies = [
+        pltpu.make_async_copy(
+            fields_v.at[pl.ds((f * per_field + c) * (tiles + 8), tiles)],
+            synced.at[f, :, pl.ds(c * LANES, LANES)],
+            sems.at[f * per_field + c],
+        )
+        for f in range(fields)
+        for c in range(per_field)
+    ]
+    for copy in copies:
+        copy.start()
     y_rows = parts.shape[1] - 1
     for r in range(y_rows + 1):
         line = parts[0, r]
@@ -233,32 +227,38 @@
             out[:, r * LANES : (r + 1) * LANES] = line * (1.0 / along_y_cells)
         else:
             out[:, r * LANES :] = line[:, :EDGE] * (1.0 / along_z_cells)
-
-
-def sum_parts(parts, tiles, slabs):
+    for copy in copies:
+        copy.wait()
+
+
+def finish(planes, parts, shape, slabs):
+    fields, tiles, cells = shape
     width = tiles * EDGE + EDGE
-    along_y_cells = EDGE * EDGE * slabs
-    along_z_cells = EDGE * EDGE * tiles * slabs
+    vmem = pl.BlockSpec(memory_space=pltpu.VMEM)
     return pl.pallas_call(
-        lambda p, o: sum_kernel(along_y_cells, along_z_cells, p, o),
-        out_shape=jax.ShapeDtypeStruct((1, width), jnp.float32),
-        in_specs=[pl.BlockSpec(memory_space=pltpu.VMEM)],
-        out_specs=pl.BlockSpec(memory_space=pltpu.VMEM),
-        name="sum_parts",
-    )(parts)
+        functools.partial(finish_kernel, EDGE * EDGE * slabs, EDGE * EDGE * tiles * slabs),
+        out_shape=(
+            jax.ShapeDtypeStruct(shape, jnp.float32),
+            jax.ShapeDtypeStruct((1, width), jnp.float32),
+        ),
+        in_specs=[vmem, vmem],
+        out_specs=(pl.BlockSpec(memory_space=pltpu.HBM), vmem),
+        scratch_shapes=[pltpu.SemaphoreType.DMA((fields * cells // LANES,))],
+        compiler_params=pltpu.CompilerParams(vmem_limit_bytes=4 * 2**20),
+        name="sum_and_write",
+    )(planes, parts)
 
 
 def shards(coarse_fields, fine_fields, owner, target_tile, tags):
-    tiles = coarse_fields.shape[0]
     blocks = lax.axis_size("blk")
     slabs = lax.axis_size("sig")
     sent = pack(owner[:, 0], target_tile[:, 0], fine_fields, blocks)
     got = lax.all_to_all(sent, "blk", split_axis=0, concat_axis=0, tiled=True)
     got = got.reshape(-1, LANES)
     coarse = jnp.transpose(coarse_fields, (1, 0, 2))
-    synced, parts = tile_step(got, coarse, tags, slabs)
+    planes, parts = tile_step(got, coarse, tags, slabs)
     parts = lax.all_to_all(parts, "sig", split_axis=0, concat_axis=0, tiled=True)
-    signature = sum_parts(parts, tiles, slabs)
+    synced, signature = finish(planes, parts, coarse.shape, slabs)
     return (jnp.transpose(synced, (1, 0, 2)), signature)
 
 

time: 68.1 us -> 67 us (0.984)
  Pallas kernels: 6.57 us -> 5.51 us
    pallas_call x2, Pallas kernels: 4.1 us -> 3.08 us  [the longest x1 1.56 us: finish(): pl.pallas_call(functools.partial(finish_kernel, EDGE * EDGE * slabs, EDGE...]
where the time goes in v3:
time: 67 us; the launch traced here: 66.8 us
  blocking collectives  60.6 us (90%)
  Pallas kernels  5.51 us (8%)
    all_to_all x1, blocking collectives, shards(): got = lax.all_to_all(sent, 'blk', split_axis=0, concat_axis=0, tiled=True)  37.8 us
    all_to_all x1, blocking collectives, shards(): lax.all_to_all(parts, 'sig', split_axis=0, concat_axis=0, tiled=True)  22.8 us
    pallas_call x1, Pallas kernels, pack(): pl.pallas_call(pack_kernel, out_shape=jax.ShapeDtypeStruct((blocks, CAP *...  2.43 us
    pallas_call x1, Pallas kernels, finish(): pl.pallas_call(functools.partial(finish_kernel, EDGE * EDGE * slabs, EDGE...  1.56 us
    pallas_call x1, Pallas kernels, tile_step(): pl.pallas_call(tile_kernel, out_shape=(jax.ShapeDtypeStruct(((slot_rows +...  1.52 us

profile of v3, /device:TPU:2, one launch (start us, length us, event | category | flops | bytes accessed | tf_op | source)
XLA Modules:
  0.0 66.8 jit_solution(10816885277195265930)
XLA Ops:
  0.6 2.4 %pack_patches.1 = f32[64,25,1,128]{3,2,1,0:T(1,128)} custom-call(s32[32]{0:T(128)} %bitcast.7, s32[32]{0:T(128)} %bitcast.8, f32[32,3,8,512]{3,2,1,0:T(8,128)} %fine.1), custom_call_target="tpu_custom_call" | custom-call | tf_op jit(solution)/shard_map/pack_patches/pallas_call | solution.py:78
  3.1 0.0 copy-start
  3.1 0.0 copy-start.1
  3.1 37.8 %all_to_all.10 = f32[64,25,1,128]{3,2,1,0:T(1,128)S(1)} all-to-all(f32[64,25,1,128]{3,2,1,0:T(1,128)} %pack_patches.1), channel_id=1, replica_groups=mesh['blk'=64,'sig'=12] {'blk'}, dimensions={0} | all-to-all | bytes 1638400 | tf_op jit(solution)/shard_map/all_to_all | solution.py:256
  40.9 0.0 copy-done
  40.9 0.0 copy-done.1
  40.9 1.5 %tile_step.1 = (f32[1768,128]{1,0:T(8,128)S(1)}, f32[12,9,1,128]{3,2,1,0:T(1,128)S(1)}) custom-call(f32[1600,128]{1,0:T(8,128)S(1)} %bitcast.5, f32[3,128,512]{2,1,0:T(8,128)S(1)} %bitcast.6, s32[128,512]{1,0:T(8,128)S(1)} %copy-done.1), custom_call_target="tpu_custom_call" | custom-call | tf_op jit(solution)/shard_map/tile_step/pallas_call | solution.py:191
  42.4 22.8 %all_to_all.11.parts = f32[12,9,1,128]{3,2,1,0:T(1,128)S(1)} all-to-all(f32[12,9,1,128]{3,2,1,0:T(1,128)S(1)} %get-tuple-element.7), channel_id=1, replica_groups=mesh['blk'=64,'sig'=12] {'sig'}, dimensions={0} | all-to-all | bytes 110592 | tf_op jit(solution)/shard_map/all_to_all | solution.py:260
  65.2 1.6 %sum_and_write.1 = (f32[3,128,512]{2,1,0:T(8,128)}, f32[1,1032]{1,0:T(1,128)}) custom-call(f32[1768,128]{1,0:T(8,128)S(1)} %get-tuple-element.6.fields_v, f32[12,9,1,128]{3,2,1,0:T(1,128)S(1)} %all_to_all.11.parts), custom_call_target="tpu_custom_call" | custom-call | tf_op jit(solution)/shard_map/sum_and_write/pallas_call | solution.py:238
Async XLA Ops:
  3.1 37.8 %copy-start = (f32[128,3,512]{2,0,1:T(8,128)S(1)}, f32[128,3,512]{2,0,1:T(8,128)}, u32[]{:S(2)}) copy-start(f32[128,3,512]{2,0,1:T(8,128)} %param.5) | copy-start | bytes 2359300
  3.1 37.8 %copy-start.1 = (s32[128,512]{1,0:T(8,128)S(1)}, s32[128,512]{1,0:T(8,128)}, u32[]{:S(2)}) copy-start(s32[128,512]{1,0:T(8,128)} %tags.1) | copy-start | bytes 786436

commit v4 on v3

--- a/solution.py
+++ b/solution.py
@@ -13,7 +13,7 @@
 CHUNKS = (3, 3, 1, 1)
 
 
-def pack_kernel(owner, target, fine, out, buf, means, marks, owner_s, target_s, count, sems):
+def pack_kernel(tiles, places, fine, out, buf, places_s, count, sems):
     patches, fields, children, cells = fine.shape
     chunk = patches // sum(CHUNKS)
     ends = [chunk * sum(CHUNKS[: k + 1]) for k in range(len(CHUNKS))]
@@ -26,72 +26,53 @@
         part = pl.ds(starts[k], ends[k] - starts[k])
         return pltpu.make_async_copy(fine.at[part], buf.at[part], sems.at[k])
 
-    owner_copy = pltpu.make_async_copy(owner, owner_s, sems.at[len(CHUNKS)])
-    target_copy = pltpu.make_async_copy(target, target_s, sems.at[len(CHUNKS) + 1])
-    owner_copy.start()
-    target_copy.start()
+    places_copy = pltpu.make_async_copy(places, places_s, sems.at[len(CHUNKS)])
+    places_copy.start()
     for k in range(len(CHUNKS)):
         fetch(k).start()
     lane = lax.broadcasted_iota(jnp.int32, (1, LANES), 1)
     own_lane = CAP * lax.axis_index("blk")
     for o in range(blocks):
         count[o] = 0
-        marks[o] = jnp.zeros((1, LANES), jnp.float32)
-    owner_copy.wait()
-    target_copy.wait()
+        out[o, CAP * slot_rows] = jnp.zeros((1, LANES), jnp.float32)
+    places_copy.wait()
     slots = []
     for i in range(patches):
-        o = owner_s[i]
+        o = places_s[i] // tiles
         rank = count[o]
         count[o] = rank + 1
-        mark = (target_s[i] + 1).astype(jnp.float32)
-        marks[o] = jnp.where(lane == own_lane + rank, mark, marks[o])
-        slots.append((o, rank))
-    leave_marks = pltpu.make_async_copy(marks, out.at[:, CAP * slot_rows], sems.at[len(CHUNKS) + 2])
-    leave_marks.start()
-
-    def leave(i):
-        o, rank = slots[i]
-        return pltpu.make_async_copy(
-            means.at[pl.ds(i * slot_rows, slot_rows)],
-            out.at[o, pl.ds(rank * slot_rows, slot_rows)],
-            sems.at[len(CHUNKS) + 3 + i],
-        )
-
+        mark = (places_s[i] - o * tiles + 1).astype(jnp.float32)
+        row = CAP * slot_rows
+        out[o, row] = jnp.where(lane == own_lane + rank, mark, out[o, row])
+        slots.append((o, rank * slot_rows))
     for k in range(len(CHUNKS)):
         fetch(k).wait()
         for i in range(starts[k], ends[k]):
+            o, row = slots[i]
             for f in range(fields):
                 mean = 0.125 * jnp.sum(buf[i, f], axis=0, keepdims=True)
                 for c in range(per_field):
-                    means[i * slot_rows + f * per_field + c] = mean[:, c * LANES : (c + 1) * LANES]
-            leave(i).start()
-    leave_marks.wait()
-    for i in range(patches):
-        leave(i).wait()
-
-
-def pack(owner, target, fine, blocks):
+                    out[o, row + f * per_field + c] = mean[:, c * LANES : (c + 1) * LANES]
+
+
+def pack(places, fine, blocks, tiles):
     patches, fields, children, cells = fine.shape
     slot_rows = fields * cells // LANES
     hbm = pl.BlockSpec(memory_space=pltpu.HBM)
     return pl.pallas_call(
-        pack_kernel,
+        functools.partial(pack_kernel, tiles),
         out_shape=jax.ShapeDtypeStruct((blocks, CAP * slot_rows + 1, 1, LANES), jnp.float32),
-        in_specs=[hbm, hbm, hbm],
-        out_specs=hbm,
+        in_specs=[pl.BlockSpec(memory_space=pl.ANY), hbm],
+        out_specs=pl.BlockSpec(memory_space=pltpu.VMEM),
         scratch_shapes=[
             pltpu.VMEM(fine.shape, jnp.float32),
-            pltpu.VMEM((patches * slot_rows, 1, LANES), jnp.float32),
-            pltpu.VMEM((blocks, 1, LANES), jnp.float32),
-            pltpu.SMEM((patches,), jnp.int32),
             pltpu.SMEM((patches,), jnp.int32),
             pltpu.SMEM((blocks,), jnp.int32),
-            pltpu.SemaphoreType.DMA((len(CHUNKS) + 3 + patches,)),
+            pltpu.SemaphoreType.DMA((len(CHUNKS) + 1,)),
         ],
-        compiler_params=pltpu.CompilerParams(vmem_limit_bytes=64 * 2**20 - 2**17),
+        compiler_params=pltpu.CompilerParams(vmem_limit_bytes=int(52.5 * 2**20)),
         name="pack_patches",
-    )(owner, target, fine)
+    )(places, fine)
 
 
 def tile_kernel(got, coarse, tags, fields_v, parts, weight_v):
@@ -204,7 +185,7 @@
     )(got, coarse, tags)
 
 
-def finish_kernel(along_y_cells, along_z_cells, fields_v, parts, synced, out, sems):
+def finish_kernel(along_y_cells, along_z_cells, fields_v, parts, synced, signature, out, sems):
     fields, tiles, cells = synced.shape
     per_field = cells // LANES
     copies = [
@@ -227,14 +208,18 @@
             out[:, r * LANES : (r + 1) * LANES] = line * (1.0 / along_y_cells)
         else:
             out[:, r * LANES :] = line[:, :EDGE] * (1.0 / along_z_cells)
+    last = pltpu.make_async_copy(out, signature, sems.at[len(copies)])
+    last.start()
     for copy in copies:
         copy.wait()
+    last.wait()
 
 
 def finish(planes, parts, shape, slabs):
     fields, tiles, cells = shape
     width = tiles * EDGE + EDGE
     vmem = pl.BlockSpec(memory_space=pltpu.VMEM)
+    hbm = pl.BlockSpec(memory_space=pltpu.HBM)
     return pl.pallas_call(
         functools.partial(finish_kernel, EDGE * EDGE * slabs, EDGE * EDGE * tiles * slabs),
         out_shape=(
@@ -242,8 +227,11 @@
             jax.ShapeDtypeStruct((1, width), jnp.float32),
         ),
         in_specs=[vmem, vmem],
-        out_specs=(pl.BlockSpec(memory_space=pltpu.HBM), vmem),
-        scratch_shapes=[pltpu.SemaphoreType.DMA((fields * cells // LANES,))],
+        out_specs=(hbm, hbm),
+        scratch_shapes=[
+            pltpu.VMEM((1, width), jnp.float32),
+            pltpu.SemaphoreType.DMA((fields * cells // LANES + 1,)),
+        ],
         compiler_params=pltpu.CompilerParams(vmem_limit_bytes=4 * 2**20),
         name="sum_and_write",
     )(planes, parts)
@@ -252,7 +240,9 @@
 def shards(coarse_fields, fine_fields, owner, target_tile, tags):
     blocks = lax.axis_size("blk")
     slabs = lax.axis_size("sig")
-    sent = pack(owner[:, 0], target_tile[:, 0], fine_fields, blocks)
+    tiles = coarse_fields.shape[0]
+    places = owner[:, 0] * tiles + target_tile[:, 0]
+    sent = pack(places, fine_fields, blocks, tiles)
     got = lax.all_to_all(sent, "blk", split_axis=0, concat_axis=0, tiled=True)
     got = got.reshape(-1, LANES)
     coarse = jnp.transpose(coarse_fields, (1, 0, 2))

time: 67 us -> 65.9 us (0.984)
  Pallas kernels: 5.51 us -> 4.13 us
  other arithmetic: 0 us -> 0.68 us
    all_to_all x1, blocking collectives: 37.8 us -> 36.8 us  [shards(): got = lax.all_to_all(sent, 'blk', split_axis=0, concat_axis=0, tiled=True)]
    pallas_call x1, Pallas kernels: 2.43 us -> 1.62 us  [pack(): pl.pallas_call(functools.partial(pack_kernel, tiles), out_shape=jax.Shape...]
    add x0 -> x1, other arithmetic: none -> 0.68 us  [shards(): places = owner[:, 0] * tiles + target_tile[:, 0]]
where the time goes in v4:
time: 65.9 us; the launch traced here: 65.7 us
  blocking collectives  60.2 us (91%)
  Pallas kernels  4.13 us (6%)
  other arithmetic  0.68 us (1%)
    all_to_all x1, blocking collectives, shards(): got = lax.all_to_all(sent, 'blk', split_axis=0, concat_axis=0, tiled=True)  36.8 us
    all_to_all x1, blocking collectives, shards(): lax.all_to_all(parts, 'sig', split_axis=0, concat_axis=0, tiled=True)  23.4 us
    pallas_call x1, Pallas kernels, pack(): pl.pallas_call(functools.partial(pack_kernel, tiles), out_shape=jax.Shape...  1.62 us
    pallas_call x1, Pallas kernels, tile_step(): pl.pallas_call(tile_kernel, out_shape=(jax.ShapeDtypeStruct(((slot_rows +...  1.53 us

profile of v4, /device:TPU:2, one launch (start us, length us, event | category | flops | bytes accessed | tf_op | source)
XLA Modules:
  0.0 65.7 jit_solution(16007186029599994212)
XLA Ops:
  0.6 0.7 %add_bitcast_fusion.places = s32[32]{0:T(128)S(1)} fusion(s32[32,1]{0,1:T(1,128)} %param.8, s32[32,1]{0,1:T(1,128)} %param.7), kind=kLoop, calls=%fused_computation | loop fusion | flops 64 | bytes 384 | tf_op jit(solution)/shard_map/add | solution.py:244
  1.3 0.0 copy-start
  1.3 0.0 copy-start.1
  1.3 1.6 %pack_patches.1 = f32[64,25,1,128]{3,2,1,0:T(1,128)S(1)} custom-call(s32[32]{0:T(128)S(1)} %add_bitcast_fusion.places, f32[32,3,8,512]{3,2,1,0:T(8,128)} %fine.1), custom_call_target="tpu_custom_call" | custom-call | tf_op jit(solution)/shard_map/pack_patches/pallas_call | solution.py:62
  2.9 36.8 %all_to_all.10 = f32[64,25,1,128]{3,2,1,0:T(1,128)S(1)} all-to-all(f32[64,25,1,128]{3,2,1,0:T(1,128)S(1)} %pack_patches.1), channel_id=1, replica_groups=mesh['blk'=64,'sig'=12] {'blk'}, dimensions={0} | all-to-all | bytes 1638400 | tf_op jit(solution)/shard_map/all_to_all | solution.py:246
  39.7 0.0 copy-done
  39.7 0.0 copy-done.1
  39.7 1.5 %tile_step.1 = (f32[1768,128]{1,0:T(8,128)S(1)}, f32[12,9,1,128]{3,2,1,0:T(1,128)S(1)}) custom-call(f32[1600,128]{1,0:T(8,128)S(1)} %bitcast.5, f32[3,128,512]{2,1,0:T(8,128)S(1)} %bitcast.6, s32[128,512]{1,0:T(8,128)S(1)} %copy-done.1), custom_call_target="tpu_custom_call" | custom-call | tf_op jit(solution)/shard_map/tile_step/pallas_call | solution.py:172
  41.3 23.4 %all_to_all.11.parts = f32[12,9,1,128]{3,2,1,0:T(1,128)S(1)} all-to-all(f32[12,9,1,128]{3,2,1,0:T(1,128)S(1)} %get-tuple-element.7), channel_id=1, replica_groups=mesh['blk'=64,'sig'=12] {'sig'}, dimensions={0} | all-to-all | bytes 110592 | tf_op jit(solution)/shard_map/all_to_all | solution.py:250
  64.7 1.0 %sum_and_write.1 = (f32[3,128,512]{2,1,0:T(8,128)}, f32[1,1032]{1,0:T(1,128)}) custom-call(f32[1768,128]{1,0:T(8,128)S(1)} %get-tuple-element.6.fields_v, f32[12,9,1,128]{3,2,1,0:T(1,128)S(1)} %all_to_all.11.parts), custom_call_target="tpu_custom_call" | custom-call | tf_op jit(solution)/shard_map/sum_and_write/pallas_call | solution.py:223
Async XLA Ops:
  1.3 38.4 %copy-start = (f32[128,3,512]{2,0,1:T(8,128)S(1)}, f32[128,3,512]{2,0,1:T(8,128)}, u32[]{:S(2)}) copy-start(f32[128,3,512]{2,0,1:T(8,128)} %param.5) | copy-start | bytes 2359300
  1.3 38.4 %copy-start.1 = (s32[128,512]{1,0:T(8,128)S(1)}, s32[128,512]{1,0:T(8,128)}, u32[]{:S(2)}) copy-start(s32[128,512]{1,0:T(8,128)} %tags.1) | copy-start | bytes 786436

commit v5 on v4

--- a/solution.py
+++ b/solution.py
@@ -75,7 +75,7 @@
     )(places, fine)
 
 
-def tile_kernel(got, coarse, tags, fields_v, parts, weight_v):
+def tile_kernel(got, coarse, tags, fields_v, parts, weight_v, ahead_v):
     fields, tiles, cells = coarse.shape
     per_field = cells // LANES
     slot_rows = fields * per_field
@@ -108,9 +108,6 @@
     z = lane % EDGE
     y = (lane // EDGE) % EDGE
     upper = lane >= EDGE * EDGE
-    inner_z = (z > 0) & (z < EDGE - 1)
-    inner_y = (y > 0) & (y < EDGE - 1)
-    total = jnp.zeros((EDGE, LANES), jnp.float32)
     for g in range(tiles // 8):
         rows = pl.ds(g * 8, 8)
         sum_z = [None] * per_field
@@ -126,19 +123,30 @@
                 if c:
                     dx = v[c] - v[c - 1]
                     sum_x[c - 1] = dx * dx if f == 0 else sum_x[c - 1] + dx * dx
-        turned = [pltpu.roll(s, EDGE * EDGE, 1) for s in sum_x]
-        weight = None
+        tag = [tags[rows, c * LANES : (c + 1) * LANES].astype(jnp.float32) for c in range(per_field)]
+        half = [pltpu.roll(s, EDGE * EDGE, 1) for s in tag]
+        by_x = by_y = by_z = None
         for c in range(per_field):
-            along_z = jnp.where(inner_z, pltpu.roll(sum_z[c], LANES - 1, 1), 0.0)
-            along_y = jnp.where(inner_y, pltpu.roll(sum_y[c], LANES - EDGE, 1), 0.0)
-            above = turned[c] if c < per_field - 1 else jnp.zeros_like(along_z)
-            below = turned[c - 1] if c else jnp.zeros_like(along_z)
-            along_x = jnp.where(upper, above, below)
-            tag = tags[rows, c * LANES : (c + 1) * LANES].astype(jnp.float32)
-            term = tag * (along_x + along_y + along_z)
-            weight = term if c == 0 else weight + term
+            tag_y = jnp.where(y >= 2, pltpu.roll(tag[c], EDGE, 1), 0.0)
+            tag_z = jnp.where(z >= 2, pltpu.roll(tag[c], 1, 1), 0.0)
+            by_y = tag_y * sum_y[c] if c == 0 else by_y + tag_y * sum_y[c]
+            by_z = tag_z * sum_z[c] if c == 0 else by_z + tag_z * sum_z[c]
+            if c:
+                term = jnp.where(upper, half[c], half[c - 1]) * sum_x[c - 1]
+                by_x = term if c == 1 else by_x + term
+        weight_v[rows] = by_x
+        ahead_v[0, rows] = by_y
+        ahead_v[1, rows] = by_z
+    total = None
+    for g in range(tiles // 8):
+        rows = pl.ds(g * 8, 8)
+        weight = (
+            weight_v[rows]
+            + pltpu.roll(ahead_v[0, rows], LANES - EDGE, 1)
+            + pltpu.roll(ahead_v[1, rows], LANES - 1, 1)
+        )
         weight_v[rows] = weight
-        total = total + weight
+        total = weight if g == 0 else total + weight
     weight_v[pl.ds(tiles, 8)] = total
 
     src = lax.broadcasted_iota(jnp.int32, (LANES, LANES), 0)
@@ -179,6 +187,7 @@
         out_specs=(vmem, vmem),
         scratch_shapes=[
             pltpu.VMEM((tiles + 8, LANES), jnp.float32),
+            pltpu.VMEM((2, tiles, LANES), jnp.float32),
         ],
         compiler_params=pltpu.CompilerParams(vmem_limit_bytes=16 * 2**20),
         name="tile_step",

time: 65.9 us -> 65.6 us (level)
  no operation moved by 1% of the time
where the time goes in v5:
time: 65.6 us; the launch traced here: 65.4 us
  blocking collectives  60.2 us (92%)
  Pallas kernels  3.87 us (6%)
  other arithmetic  0.68 us (1%)
    all_to_all x1, blocking collectives, shards(): got = lax.all_to_all(sent, 'blk', split_axis=0, concat_axis=0, tiled=True)  36.8 us
    all_to_all x1, blocking collectives, shards(): lax.all_to_all(parts, 'sig', split_axis=0, concat_axis=0, tiled=True)  23.4 us
    pallas_call x1, Pallas kernels, pack(): pl.pallas_call(functools.partial(pack_kernel, tiles), out_shape=jax.Shape...  1.62 us

profile of v5, /device:TPU:2, one launch (start us, length us, event | category | flops | bytes accessed | tf_op | source)
XLA Modules:
  0.0 65.4 jit_solution(7176360109314005745)
XLA Ops:
  0.6 0.7 %add_bitcast_fusion.places = s32[32]{0:T(128)S(1)} fusion(s32[32,1]{0,1:T(1,128)} %param.8, s32[32,1]{0,1:T(1,128)} %param.7), kind=kLoop, calls=%fused_computation | loop fusion | flops 64 | bytes 384 | tf_op jit(solution)/shard_map/add | solution.py:253
  1.3 0.0 copy-start
  1.3 0.0 copy-start.1
  1.3 1.6 %pack_patches.1 = f32[64,25,1,128]{3,2,1,0:T(1,128)S(1)} custom-call(s32[32]{0:T(128)S(1)} %add_bitcast_fusion.places, f32[32,3,8,512]{3,2,1,0:T(8,128)} %fine.1), custom_call_target="tpu_custom_call" | custom-call | tf_op jit(solution)/shard_map/pack_patches/pallas_call | solution.py:62
  2.9 36.8 %all_to_all.10 = f32[64,25,1,128]{3,2,1,0:T(1,128)S(1)} all-to-all(f32[64,25,1,128]{3,2,1,0:T(1,128)S(1)} %pack_patches.1), channel_id=1, replica_groups=mesh['blk'=64,'sig'=12] {'blk'}, dimensions={0} | all-to-all | bytes 1638400 | tf_op jit(solution)/shard_map/all_to_all | solution.py:255
  39.7 0.0 copy-done
  39.7 0.0 copy-done.1
  39.7 1.3 %tile_step.1 = (f32[1768,128]{1,0:T(8,128)S(1)}, f32[12,9,1,128]{3,2,1,0:T(1,128)S(1)}) custom-call(f32[1600,128]{1,0:T(8,128)S(1)} %bitcast.5, f32[3,128,512]{2,1,0:T(8,128)S(1)} %bitcast.6, s32[128,512]{1,0:T(8,128)S(1)} %copy-done.1), custom_call_target="tpu_custom_call" | custom-call | tf_op jit(solution)/shard_map/tile_step/pallas_call | solution.py:180
  41.0 23.4 %all_to_all.11.parts = f32[12,9,1,128]{3,2,1,0:T(1,128)S(1)} all-to-all(f32[12,9,1,128]{3,2,1,0:T(1,128)S(1)} %get-tuple-element.7), channel_id=1, replica_groups=mesh['blk'=64,'sig'=12] {'sig'}, dimensions={0} | all-to-all | bytes 110592 | tf_op jit(solution)/shard_map/all_to_all | solution.py:259
  64.4 1.0 %sum_and_write.1 = (f32[3,128,512]{2,1,0:T(8,128)}, f32[1,1032]{1,0:T(1,128)}) custom-call(f32[1768,128]{1,0:T(8,128)S(1)} %get-tuple-element.6.fields_v, f32[12,9,1,128]{3,2,1,0:T(1,128)S(1)} %all_to_all.11.parts), custom_call_target="tpu_custom_call" | custom-call | tf_op jit(solution)/shard_map/sum_and_write/pallas_call | solution.py:232
Async XLA Ops:
  1.3 38.4 %copy-start = (f32[128,3,512]{2,0,1:T(8,128)S(1)}, f32[128,3,512]{2,0,1:T(8,128)}, u32[]{:S(2)}) copy-start(f32[128,3,512]{2,0,1:T(8,128)} %param.5) | copy-start | bytes 2359300
  1.3 38.4 %copy-start.1 = (s32[128,512]{1,0:T(8,128)S(1)}, s32[128,512]{1,0:T(8,128)}, u32[]{:S(2)}) copy-start(s32[128,512]{1,0:T(8,128)} %tags.1) | copy-start | bytes 786436

commit v6 on v5

--- a/solution.py
+++ b/solution.py
@@ -75,7 +75,7 @@
     )(places, fine)
 
 
-def tile_kernel(got, coarse, tags, fields_v, parts, weight_v, ahead_v):
+def tile_kernel(got, coarse, tags, merged, parts, fields_v, weight_v, ahead_v):
     fields, tiles, cells = coarse.shape
     per_field = cells // LANES
     slot_rows = fields * per_field
@@ -116,6 +116,7 @@
         for f in range(fields):
             v = [fields_v[pl.ds((f * per_field + c) * pitch + g * 8, 8)] for c in range(per_field)]
             for c in range(per_field):
+                merged[f, rows, c * LANES : (c + 1) * LANES] = v[c]
                 dz = v[c] - pltpu.roll(v[c], 2, 1)
                 dy = v[c] - pltpu.roll(v[c], 2 * EDGE, 1)
                 sum_z[c] = dz * dz if f == 0 else sum_z[c] + dz * dz
@@ -180,12 +181,13 @@
     return pl.pallas_call(
         tile_kernel,
         out_shape=(
-            jax.ShapeDtypeStruct(((slot_rows + 1) * (tiles + 8), LANES), jnp.float32),
+            jax.ShapeDtypeStruct(coarse.shape, jnp.float32),
             jax.ShapeDtypeStruct((slabs, part_rows, 1, LANES), jnp.float32),
         ),
         in_specs=[vmem, vmem, vmem],
         out_specs=(vmem, vmem),
         scratch_shapes=[
+            pltpu.VMEM(((slot_rows + 1) * (tiles + 8), LANES), jnp.float32),
             pltpu.VMEM((tiles + 8, LANES), jnp.float32),
             pltpu.VMEM((2, tiles, LANES), jnp.float32),
         ],
@@ -194,20 +196,9 @@
     )(got, coarse, tags)
 
 
-def finish_kernel(along_y_cells, along_z_cells, fields_v, parts, synced, signature, out, sems):
-    fields, tiles, cells = synced.shape
-    per_field = cells // LANES
-    copies = [
-        pltpu.make_async_copy(
-            fields_v.at[pl.ds((f * per_field + c) * (tiles + 8), tiles)],
-            synced.at[f, :, pl.ds(c * LANES, LANES)],
-            sems.at[f * per_field + c],
-        )
-        for f in range(fields)
-        for c in range(per_field)
-    ]
-    for copy in copies:
-        copy.start()
+def finish_kernel(along_y_cells, along_z_cells, merged, parts, synced, signature, out, sems):
+    tiles_copy = pltpu.make_async_copy(merged, synced, sems.at[0])
+    tiles_copy.start()
     y_rows = parts.shape[1] - 1
     for r in range(y_rows + 1):
         line = parts[0, r]
@@ -217,33 +208,32 @@
             out[:, r * LANES : (r + 1) * LANES] = line * (1.0 / along_y_cells)
         else:
             out[:, r * LANES :] = line[:, :EDGE] * (1.0 / along_z_cells)
-    last = pltpu.make_async_copy(out, signature, sems.at[len(copies)])
+    last = pltpu.make_async_copy(out, signature, sems.at[1])
     last.start()
-    for copy in copies:
-        copy.wait()
+    tiles_copy.wait()
     last.wait()
 
 
-def finish(planes, parts, shape, slabs):
-    fields, tiles, cells = shape
+def finish(merged, parts, slabs):
+    tiles = merged.shape[1]
     width = tiles * EDGE + EDGE
     vmem = pl.BlockSpec(memory_space=pltpu.VMEM)
     hbm = pl.BlockSpec(memory_space=pltpu.HBM)
     return pl.pallas_call(
         functools.partial(finish_kernel, EDGE * EDGE * slabs, EDGE * EDGE * tiles * slabs),
         out_shape=(
-            jax.ShapeDtypeStruct(shape, jnp.float32),
+            jax.ShapeDtypeStruct(merged.shape, jnp.float32),
             jax.ShapeDtypeStruct((1, width), jnp.float32),
         ),
         in_specs=[vmem, vmem],
         out_specs=(hbm, hbm),
         scratch_shapes=[
             pltpu.VMEM((1, width), jnp.float32),
-            pltpu.SemaphoreType.DMA((fields * cells // LANES + 1,)),
+            pltpu.SemaphoreType.DMA((2,)),
         ],
         compiler_params=pltpu.CompilerParams(vmem_limit_bytes=4 * 2**20),
         name="sum_and_write",
-    )(planes, parts)
+    )(merged, parts)
 
 
 def shards(coarse_fields, fine_fields, owner, target_tile, tags):
@@ -255,9 +245,9 @@
     got = lax.all_to_all(sent, "blk", split_axis=0, concat_axis=0, tiled=True)
     got = got.reshape(-1, LANES)
     coarse = jnp.transpose(coarse_fields, (1, 0, 2))
-    planes, parts = tile_step(got, coarse, tags, slabs)
+    merged, parts = tile_step(got, coarse, tags, slabs)
     parts = lax.all_to_all(parts, "sig", split_axis=0, concat_axis=0, tiled=True)
-    synced, signature = finish(planes, parts, coarse.shape, slabs)
+    synced, signature = finish(merged, parts, slabs)
     return (jnp.transpose(synced, (1, 0, 2)), signature)
 
 

time: 65.6 us -> 65.6 us (level)
  no operation moved by 1% of the time
where the time goes in v6:
time: 65.6 us; the launch traced here: 65.3 us
  blocking collectives  60.2 us (92%)
  Pallas kernels  3.79 us (6%)
  other arithmetic  0.68 us (1%)
    all_to_all x1, blocking collectives, shards(): got = lax.all_to_all(sent, 'blk', split_axis=0, concat_axis=0, tiled=True)  36.8 us
    all_to_all x1, blocking collectives, shards(): lax.all_to_all(parts, 'sig', split_axis=0, concat_axis=0, tiled=True)  23.4 us
    pallas_call x1, Pallas kernels, pack(): pl.pallas_call(functools.partial(pack_kernel, tiles), out_shape=jax.Shape...  1.62 us

profile of v6, /device:TPU:2, one launch (start us, length us, event | category | flops | bytes accessed | tf_op | source)
XLA Modules:
  0.0 65.3 jit_solution(17643905058511921165)
XLA Ops:
  0.6 0.7 %add_bitcast_fusion.places = s32[32]{0:T(128)S(1)} fusion(s32[32,1]{0,1:T(1,128)} %param.8, s32[32,1]{0,1:T(1,128)} %param.7), kind=kLoop, calls=%fused_computation | loop fusion | flops 64 | bytes 384 | tf_op jit(solution)/shard_map/add | solution.py:243
  1.3 0.0 copy-start
  1.3 0.0 copy-start.1
  1.3 1.6 %pack_patches.1 = f32[64,25,1,128]{3,2,1,0:T(1,128)S(1)} custom-call(s32[32]{0:T(128)S(1)} %add_bitcast_fusion.places, f32[32,3,8,512]{3,2,1,0:T(8,128)} %fine.1), custom_call_target="tpu_custom_call" | custom-call | tf_op jit(solution)/shard_map/pack_patches/pallas_call | solution.py:62
  2.9 36.8 %all_to_all.10 = f32[64,25,1,128]{3,2,1,0:T(1,128)S(1)} all-to-all(f32[64,25,1,128]{3,2,1,0:T(1,128)S(1)} %pack_patches.1), channel_id=1, replica_groups=mesh['blk'=64,'sig'=12] {'blk'}, dimensions={0} | all-to-all | bytes 1638400 | tf_op jit(solution)/shard_map/all_to_all | solution.py:245
  39.7 0.0 copy-done
  39.7 0.0 copy-done.1
  39.7 1.3 %tile_step.1 = (f32[3,128,512]{2,1,0:T(8,128)S(1)}, f32[12,9,1,128]{3,2,1,0:T(1,128)S(1)}) custom-call(f32[1600,128]{1,0:T(8,128)S(1)} %bitcast.5, f32[3,128,512]{2,1,0:T(8,128)S(1)} %bitcast.6, s32[128,512]{1,0:T(8,128)S(1)} %copy-done.1), custom_call_target="tpu_custom_call" | custom-call | tf_op jit(solution)/shard_map/tile_step/pallas_call | solution.py:181
  41.0 23.4 %all_to_all.11.parts = f32[12,9,1,128]{3,2,1,0:T(1,128)S(1)} all-to-all(f32[12,9,1,128]{3,2,1,0:T(1,128)S(1)} %get-tuple-element.7), channel_id=1, replica_groups=mesh['blk'=64,'sig'=12] {'sig'}, dimensions={0} | all-to-all | bytes 110592 | tf_op jit(solution)/shard_map/all_to_all | solution.py:249
  64.4 0.9 %sum_and_write.1 = (f32[3,128,512]{2,1,0:T(8,128)}, f32[1,1032]{1,0:T(1,128)}) custom-call(f32[3,128,512]{2,1,0:T(8,128)S(1)} %get-tuple-element.6.merged, f32[12,9,1,128]{3,2,1,0:T(1,128)S(1)} %all_to_all.11.parts), custom_call_target="tpu_custom_call" | custom-call | tf_op jit(solution)/shard_map/sum_and_write/pallas_call | solution.py:222
Async XLA Ops:
  1.3 38.4 %copy-start = (f32[128,3,512]{2,0,1:T(8,128)S(1)}, f32[128,3,512]{2,0,1:T(8,128)}, u32[]{:S(2)}) copy-start(f32[128,3,512]{2,0,1:T(8,128)} %param.5) | copy-start | bytes 2359300
  1.3 38.4 %copy-start.1 = (s32[128,512]{1,0:T(8,128)S(1)}, s32[128,512]{1,0:T(8,128)}, u32[]{:S(2)}) copy-start(s32[128,512]{1,0:T(8,128)} %tags.1) | copy-start | bytes 786436
